TPU v7x, 32 devices: a whole 2x2x4 slice. The times are simulated.
32 devices in a mesh: row: 8 (over z, y), col: 4 (over x, core).
Axes of the slice: x: 2, y: 2, z: 4, core: 2. Of those that a mesh axis runs over, the one named last changes fastest.
Arguments:
- diag_block: float32 [256, 256], P(('row', 'col')), may hold values from -1 to 40, as said below
- panel: float32 [24576, 256], P(('row', 'col')), may hold values from -6 to 6
- trailing: bfloat16 [24576, 24576], P('row', 'col'), may hold values from -6 to 6
Outputs:
- diag_factor: float32 [256, 256], P(('row', 'col'))
- panel_factor: float32 [24576, 256], P(('row', 'col'))
- trailing_out: bfloat16 [24576, 24576], P('row', 'col')
Inputs may be any that keep to these rules, and one draw needn't show every extreme that they name: diag_block is symmetric, with off-diagonal entries in -1 to 1 and diagonal entries in 24 to 40, so it is positive definite.
All inputs are finite; a program needn't handle non-finite values.
Results may differ from a plain program's by a relative error of at most 0.001.
Values sent between devices are 32-bit elements; how exact they have to be, the bound alone decides.
A program may use at most 128 MiB of HBM per device.

v0:
```python
import jax
import jax.numpy as jnp
from jax import lax
from jax.sharding import PartitionSpec as P

BLOCK = 256


def spread(block, axis, holder):
    block = jnp.where(lax.axis_index(axis) == holder, block, jnp.zeros_like(block))
    return lax.psum(block, axis)


def per_device(diag_block, panel, trailing):
    whole_diag = lax.all_gather(diag_block, ("row", "col"), axis=0, tiled=True)
    panel_width = whole_diag.shape[0]
    diag_factor = jnp.linalg.cholesky(whole_diag)
    identity = jnp.eye(panel_width, dtype=jnp.float32)
    inverse = lax.linalg.triangular_solve(diag_factor, identity, left_side=True, lower=True)
    panel_factor = jnp.dot(
        panel, inverse.T, precision=lax.Precision.HIGHEST, preferred_element_type=jnp.float32
    )
    diag_share = panel_width // lax.axis_size(("row", "col"))
    factor_rows = lax.dynamic_slice_in_dim(
        diag_factor, lax.axis_index(("row", "col")) * diag_share, diag_share, 0
    )
    row_panel = lax.all_gather(panel_factor, "col", axis=0, tiled=True)
    count_cols = lax.axis_size("col")
    column_ratio = lax.axis_size("row") // count_cols
    column_index = lax.axis_index("col")
    local_rows = row_panel.shape[0]
    per_block = local_rows // BLOCK
    owners = jnp.stack(
        [
            spread(row_panel, "row", owner_turn * count_cols + column_index)
            for owner_turn in range(column_ratio)
        ]
    )
    owners = owners.reshape(column_ratio, per_block, BLOCK, panel_width)
    column_panel = jnp.transpose(owners, (1, 0, 2, 3)).reshape(
        column_ratio * local_rows, panel_width
    )
    update = jnp.dot(
        row_panel,
        column_panel.T,
        precision=lax.Precision.HIGHEST,
        preferred_element_type=jnp.float32,
    )
    trailing_out = (trailing.astype(jnp.float32) - update).astype(jnp.bfloat16)
    return (factor_rows, panel_factor, trailing_out)


def solution(mesh):
    placed = (P(("row", "col"), None), P(("row", "col"), None), P("row", "col"))
    return jax.shard_map(
        per_device,
        mesh=mesh,
        in_specs=placed,
        out_specs=(P(("row", "col"), None), P(("row", "col"), None), P("row", "col")),
        check_vma=False,
    )
```

profile of v0, /device:TPU:0, one launch (start us, length us, event | category | flops | bytes accessed | tf_op | source)
XLA Modules:
  0.0 508.1 jit_solution(17961324278501280422)
XLA Ops:
  7.2 0.0 copy-start
  7.2 0.0 all-gather.2.cloned.1.call-start
  7.3 44.3 %all_gather.6 = f32[256,256]{1,0:T(8,128)S(1)} all-gather(f32[8,256]{1,0:T(8,128)} %param.3), channel_id=1, replica_groups=mesh['row'=8,'col'=4] {'row','col'}, dimensions={0}, use_global_device_ids=true | all-gather | bytes 270336 | tf_op jit(solution)/shard_map/all_gather | solution.py:15
  51.6 0.1 copy.15
  51.8 11.7 %cholesky.50 = f32[128,128]{1,0:T(8,128)S(1)} custom-call(f32[128,128]{1,0:T(8,128)S(1)} %cholesky.118), custom_call_target="Cholesky" | custom-call | tf_op jit(solution)/shard_map/jit(cholesky)/cholesky | solution.py:17
  63.5 9.8 %custom-call.14 = f32[1,128,128]{1,2,0:T(8,128)S(1)} custom-call(f32[1,128,128]{2,1,0:T(8,128)S(1)} %get-tuple-element.39), custom_call_target="InvertDiagBlocksLowerTriangular" | custom-call | tf_op jit(solution)/shard_map/jit(cholesky)/cholesky | solution.py:17
  73.4 0.2 constant_dynamic-update-slice_fusion
  73.6 0.3 convolution_subtract_fusion.1
  73.9 11.7 %cholesky.105 = f32[128,128]{1,0:T(8,128)S(1)} custom-call(f32[128,128]{1,0:T(8,128)S(1)} %convolution_subtract_fusion.1), custom_call_target="Cholesky" | custom-call | tf_op jit(solution)/shard_map/jit(cholesky)/cholesky | solution.py:17
  85.6 0.6 compare_reduce_fusion
  87.6 0.1 triangular_solve.44
  87.7 4.1 while.1
  87.8 0.6 fusion.22
  88.4 1.4 bitcast_dynamic-update-slice_fusion.2
  89.8 0.6 fusion.22
  90.4 1.4 bitcast_dynamic-update-slice_fusion.2
  91.8 19.7 %custom-call.15 = f32[2,128,128]{1,2,0:T(8,128)S(1)} custom-call(f32[2,128,128]{2,1,0:T(8,128)S(1)} %get-tuple-element.10), custom_call_target="InvertDiagBlocksLowerTriangular" | custom-call | tf_op jit(solution)/shard_map/triangular_solve | solution.py:19
  111.5 0.3 fusion.5
  111.8 0.3 convolution_subtract_fusion
  112.0 0.3 fusion.8
  112.3 0.0 copy-done
  112.4 1.7 convolution_bitcast_fusion
  114.1 0.0 all-gather.2.cloned.1.call-update
  114.1 0.0 all-reduce.4.cloned.1.call-start
  114.2 24.7 %all-gather.2.cloned.1.call-done = f32[3072,256]{0,1:T(8,128)} async-done(((f32[768,256]{0,1:T(8,128)}), f32[3072,256]{0,1:T(8,128)}) %all-gather.2.cloned.1.call-update) | async-done | bytes 3145744 | tf_op jit(solution)/shard_map/all_gather | solution.py:27
  138.9 5.5 %broadcast_select_fusion.1 = (f32[3072,256]{0,1:T(8,128)}, f32[3072,256]{0,1:T(8,128)}) fusion(f32[3072,256]{0,1:T(8,128)} %all-gather.2.cloned.1.call-done, pred[]{:T(512)S(6)} %eq.12, pred[]{:T(512)S(6)} %eq.13), kind=kLoop, calls=%fused_computation.5 | loop fusion | flops 1572864 | bytes 9437186 | tf_op jit(solution)/shard_map/jit(_where)/select_n | solution.py:10
  144.4 3.6 copy.16
  147.9 3.5 copy.17
  151.4 0.0 copy-start.3
  151.4 0.0 all-reduce.4.cloned.1.call-update
  151.5 1.1 copy-done.3
  152.6 1.1 copy.19
  153.7 0.6 constant_dynamic-slice_fusion.1
  154.3 209.7 %all-reduce.4.cloned.1.call-done = (f32[1,12,256,256]{3,2,1,0:T(8,128)}, f32[1,12,256,256]{3,2,1,0:T(8,128)}) async-done(((f32[1,12,256,256]{3,2,1,0:T(8,128)}, f32[1,12,256,256]{3,2,1,0:T(8,128)}), (f32[1,12,256,256]{3,2,1,0:T(8,128)}, f32[1,12,256,256]{3,2,1,0:T(8,128)})) %all-reduce.4.cloned.1.call-update) | async-done | bytes 6291472 | tf_op jit(solution)/shard_map/psum | solution.py:11
  364.0 3.5 maximum_bitcast_fusion
  367.5 0.0 copy-start.2
  367.5 0.6 copy.18
  368.1 1.3 copy-done.2
  369.4 0.0 copy-start.1
  369.4 131.8 %subtract_convert_fusion = bf16[3072,6144]{1,0:T(8,128)(2,1)} fusion(bf16[3072,6144]{1,0:T(8,128)(2,1)} %param.5, f32[3072,256]{0,1:T(8,128)S(1)} %copy-done.2, f32[6144,256]{1,0:T(8,128)S(1)} %bitcast.41), kind=kOutput, calls=%fused_computation.2 | convolution fusion | flops 58038681600 | bytes 84934656 | tf_op jit(solution)/shard_map/dot_general | solution.py:43
  501.2 0.0 copy-done.1
  (11 shorter events, 0.2 us)
Async XLA Ops:
  7.2 105.2 %copy-start = (f32[768,256]{1,0:T(8,128)S(1)}, f32[768,256]{1,0:T(8,128)}, u32[]{:S(2)}) copy-start(f32[768,256]{1,0:T(8,128)} %param.4) | copy-start | bytes 2359300
  7.2 131.7 %all-gather.2.cloned.1.call-start = ((), (), s32[]{:S(2)}) async-start(), calls=%async_computation | async-start | bytes 3932160 | tf_op jit(solution)/shard_map/all_gather | solution.py:27
  114.1 250.0 %all-reduce.4.cloned.1.call-start = ((), (), s32[]{:S(2)}) async-start(), calls=%async_computation.1 | async-start | bytes 12582912 | tf_op jit(solution)/shard_map/psum | solution.py:11
  151.4 1.1 copy-start.3
  367.5 1.9 copy-start.2
  369.4 131.8 %copy-start.1 = (f32[768,256]{1,0:T(8,128)S(1)}, f32[768,256]{1,0:T(8,128)}, u32[]{:S(2)}) copy-start(f32[768,256]{1,0:T(8,128)} %param.4) | copy-start | bytes 2359300
Sparse Core Ops, SparseCore 0:
  114.2 24.6 all-gather.1
  151.6 212.4 all-reduce.3
where the time goes:
time: 508 us
  waiting for transfers between devices  234 us (46%)
  matrix products  135 us (27%)
  other arithmetic  62.7 us (12%)
  blocking collectives  44.3 us (9%)
  local copies, waits for them, and re-layouts  16 us (3%)
  between operations  15.5 us (3%)
    psum x1, waiting for transfers between devices, spread(): return lax.psum(block, axis)  210 us
    dot_general x1, matrix products, per_device(): jnp.dot(row_panel, column_panel.T, precision=lax.Precision.HIGHEST, prefe...  132 us
    all_gather x1, blocking collectives, per_device(): whole_diag = lax.all_gather(diag_block, ('row', 'col'), axis=0, tiled=True)  44.3 us
    another operation x6, other arithmetic, per_device(): diag_factor = jnp.linalg.cholesky(whole_diag)  34 us
    all_gather x1, waiting for transfers between devices, per_device(): row_panel = lax.all_gather(panel_factor, 'col', axis=0, tiled=True)  24.7 us
    another operation x3, other arithmetic, per_device(): lax.linalg.triangular_solve(diag_factor, identity, left_side=True, lower=...  19.7 us
  transfers between devices with their start and end apart: 2, of which 2 were waited for; matrix products, arithmetic and copies ran while one was open for 0% of the time, Pallas kernels for 0%

commit v1 on v0

v1 whole, which is shorter than its diff:
```python
import functools

import jax
import jax.numpy as jnp
from jax import lax
from jax.experimental import pallas as pl
from jax.experimental.pallas import tpu as pltpu
from jax.sharding import PartitionSpec as P

BLOCK = 256
MIB = 1 << 20
MESH = pl.DeviceIdType.MESH


def split_three(x, axis, first):
    high = x.astype(jnp.bfloat16)
    low = (x - high.astype(jnp.float32)).astype(jnp.bfloat16)
    return jnp.concatenate([high, high, low] if first else [high, low, high], axis=axis)


def dot_last(a, b):
    return lax.dot_general(
        a, b, (((1,), (1,)), ((), ())), preferred_element_type=jnp.float32
    )


def gather_diag_kernel(n_row, n_col, mine, whole, held, send_sem, recv_sem):
    count = n_row * n_col
    me = lax.axis_index("row") * n_col + lax.axis_index("col")

    def target(step):
        other = lax.rem(me + step, count)
        return (other // n_col, lax.rem(other, n_col))

    barrier = pltpu.get_barrier_semaphore()

    def greet(step, carry):
        pl.semaphore_signal(barrier, inc=1, device_id=target(step), device_id_type=MESH)
        return carry

    lax.fori_loop(1, count, greet, 0)
    pl.semaphore_wait(barrier, count - 1)
    def send(step, carry):
        pltpu.make_async_remote_copy(
            src_ref=mine,
            dst_ref=held.at[me],
            send_sem=send_sem,
            recv_sem=recv_sem,
            device_id=target(step),
            device_id_type=MESH,
        ).start()
        return carry

    lax.fori_loop(1, count, send, 0)
    held[me] = mine[...]
    others = held.at[pl.ds(0, count - 1)]
    pltpu.make_async_copy(others, others, recv_sem).wait()
    pltpu.make_async_copy(others, others, send_sem).wait()
    whole[...] = held[...]


def gather_diag(diag_block, n_row, n_col):
    share, width = diag_block.shape
    whole = (n_row * n_col, share, width)
    gathered = pl.pallas_call(
        functools.partial(gather_diag_kernel, n_row, n_col),
        out_shape=jax.ShapeDtypeStruct(whole, jnp.float32),
        in_specs=[pl.BlockSpec(memory_space=pltpu.VMEM)],
        out_specs=pl.BlockSpec(memory_space=pltpu.VMEM),
        scratch_shapes=[
            pltpu.VMEM(whole, jnp.float32),
            pltpu.SemaphoreType.DMA,
            pltpu.SemaphoreType.DMA,
        ],
        compiler_params=pltpu.CompilerParams(collective_id=0, has_side_effects=True),
        cost_estimate=pl.CostEstimate(flops=0, bytes_accessed=16 * MIB, transcendentals=0),
        name="gather_diag",
    )(diag_block)
    return gathered.reshape(-1, width)


def eliminate(block, size):
    row_of = lax.broadcasted_iota(jnp.int32, (size, 2 * size), 0)
    col_of = lax.broadcasted_iota(jnp.int32, (size, 2 * size), 1)
    for j in range(size - 1):
        pivot_row = block[j : j + 1, :]
        scaled = pivot_row * (1.0 / block[j : j + 1, j : j + 1])
        factors = jnp.where(row_of > j, block[:, j : j + 1], 0.0)
        block = block - factors * scaled
    pivots = jnp.sum(jnp.where(row_of == col_of, block, 0.0), axis=1, keepdims=True)
    return block / jnp.sqrt(pivots)


def factor_kernel(diag, panel, lower, inverse, panel_factor, work):
    width = diag.shape[0]
    size = min(64, width)
    row_of = lax.broadcasted_iota(jnp.int32, (width, width), 0)
    col_of = lax.broadcasted_iota(jnp.int32, (width, width), 1)
    work[:, :width] = diag[...]
    work[:, width:] = jnp.where(row_of == col_of, 1.0, 0.0)
    eye = jnp.where(row_of == col_of, 1.0, 0.0)[:size, :size]
    for start in range(0, width, size):
        stop = start + size
        block = jnp.concatenate([work[start:stop, start:stop], eye], axis=1)
        small = eliminate(block, size)[:, size:]
        rows = lax.dot_general(
            small, work[start:stop, :], (((1,), (0,)), ((), ())),
            precision=lax.Precision.HIGHEST, preferred_element_type=jnp.float32,
        )
        work[start:stop, :] = rows
        if stop < width:
            work[stop:, :] -= lax.dot_general(
                rows[:, stop:width], rows, (((0,), (0,)), ((), ())),
                precision=lax.Precision.HIGHEST, preferred_element_type=jnp.float32,
            )
    lower[...] = jnp.where(row_of >= col_of, work[:, :width].T, 0.0)
    solved = work[:, width:]
    inverse[...] = solved
    panel_factor[...] = dot_last(
        split_three(panel[...], 1, False), split_three(solved, 1, True)
    )


def factor(whole_diag, panel):
    width = whole_diag.shape[0]
    square = jax.ShapeDtypeStruct((width, width), jnp.float32)
    return pl.pallas_call(
        factor_kernel,
        out_shape=(square, square, jax.ShapeDtypeStruct(panel.shape, jnp.float32)),
        in_specs=[pl.BlockSpec(memory_space=pltpu.VMEM)] * 2,
        out_specs=[pl.BlockSpec(memory_space=pltpu.VMEM)] * 3,
        scratch_shapes=[pltpu.VMEM((width, 2 * width), jnp.float32)],
        compiler_params=pltpu.CompilerParams(vmem_limit_bytes=24 * MIB),
        cost_estimate=pl.CostEstimate(
            flops=0, bytes_accessed=128 * MIB, transcendentals=0
        ),
        name="factor",
    )(whole_diag, panel)


def update_kernel(ratio, step_cols, row_raw, col_raw, inverse, trailing, out, right):
    width = inverse.shape[0]
    per_block = col_raw.shape[0] // (ratio * BLOCK)
    inverse_parts = split_three(inverse[...], 1, True)

    @pl.when(pl.program_id(0) == 0)
    def _():
        def one_block(m, carry):
            source = lax.rem(m, ratio) * per_block + m // ratio
            raw = col_raw[pl.ds(pl.multiple_of(source * BLOCK, BLOCK), BLOCK), :]
            factor_t = dot_last(inverse_parts, split_three(raw, 1, False))
            cols = pl.ds(pl.multiple_of(m * BLOCK, BLOCK), BLOCK)
            right[:, cols] = split_three(factor_t, 0, False)
            return carry

        lax.fori_loop(0, ratio * per_block, one_block, 0, unroll=2)

    left = split_three(dot_last(split_three(row_raw[...], 1, False), inverse_parts), 1, True)
    for start in range(0, trailing.shape[1], step_cols):
        cols = slice(start, start + step_cols)
        product = jnp.dot(left, right[:, cols], preferred_element_type=jnp.float32)
        out[:, cols] = (trailing[:, cols].astype(jnp.float32) - product).astype(jnp.bfloat16)


def largest(total, options):
    return next((o for o in options if total % o == 0), total)


def update(row_raw, col_raw, inverse, trailing, ratio):
    rows, cols = trailing.shape
    width = inverse.shape[0]
    tile = largest(rows, (512, 256))
    return pl.pallas_call(
        functools.partial(update_kernel, ratio, largest(cols, (512, 256))),
        grid=(rows // tile,),
        out_shape=jax.ShapeDtypeStruct((rows, cols), jnp.bfloat16),
        in_specs=[
            pl.BlockSpec((tile, width), lambda r: (r, 0)),
            pl.BlockSpec(memory_space=pltpu.VMEM),
            pl.BlockSpec(memory_space=pltpu.VMEM),
            pl.BlockSpec((tile, cols), lambda r: (r, 0)),
        ],
        out_specs=pl.BlockSpec((tile, cols), lambda r: (r, 0)),
        scratch_shapes=[pltpu.VMEM((3 * width, cols), jnp.bfloat16)],
        compiler_params=pltpu.CompilerParams(vmem_limit_bytes=56 * MIB),
        cost_estimate=pl.CostEstimate(
            flops=6 * rows * cols * width, bytes_accessed=4 * rows * cols, transcendentals=0
        ),
        name="update",
    )(row_raw, col_raw, inverse, trailing)


def per_device(diag_block, panel, trailing):
    n_row, n_col = lax.axis_size("row"), lax.axis_size("col")
    ratio = n_row // n_col
    swap = []
    for turn in range(ratio):
        for a in range(n_col):
            for b in range(n_col):
                source = (turn * n_col + a) * n_col + b
                swap.append((source, (turn * n_col + b) * n_col + a))
    column_share = lax.ppermute(panel, ("row", "col"), swap)
    column_raw = lax.all_gather(column_share, "row", axis=0, tiled=True)
    row_raw = lax.all_gather(panel, "col", axis=0, tiled=True)

    whole_diag = gather_diag(diag_block, n_row, n_col)
    lower, inverse, panel_factor = factor(whole_diag, panel)
    share = diag_block.shape[0]
    me = lax.axis_index(("row", "col"))
    factor_rows = lax.dynamic_slice_in_dim(lower, me * share, share, 0)
    trailing_out = update(row_raw, column_raw, inverse, trailing, ratio)
    return (factor_rows, panel_factor, trailing_out)


def solution(mesh):
    placed = (P(("row", "col"), None), P(("row", "col"), None), P("row", "col"))
    return jax.shard_map(
        per_device,
        mesh=mesh,
        in_specs=placed,
        out_specs=placed,
        check_vma=False,
    )
```

time: 508 us -> 210 us (0.41)
  waiting for transfers between devices: 234 us -> 82 us
  matrix products: 135 us -> 0 us
  Pallas kernels: 0 us -> 108 us
  other arithmetic: 62.7 us -> 0 us
  blocking collectives: 44.3 us -> 0 us
  local copies, waits for them, and re-layouts: 16 us -> 4.25 us
    psum x1 -> x0, waiting for transfers between devices: 210 us -> none  [spread(): return lax.psum(block, axis)]
    dot_general x2 -> x0, matrix products: 134 us -> none  [the longest x1 132 us: per_device(): jnp.dot(row_panel, column_panel.T, precision=lax.Precision.HIGHEST, prefe...]
    pallas_call x0 -> x3, Pallas kernels: none -> 108 us  [the longest x1 47.9 us: update(): pl.pallas_call(functools.partial(update_kernel, ratio, largest(cols, (512...]
    all_gather x1 -> x2, waiting for transfers between devices: 24.7 us -> 81.3 us  [the longest x1 81.3 us: per_device(): column_raw = lax.all_gather(column_share, 'row', axis=0, tiled=True)]
    another operation x9 -> x0, other arithmetic: 53.7 us -> none  [the longest x6 34 us: per_device(): diag_factor = jnp.linalg.cholesky(whole_diag)]
    all_gather x1 -> x0, blocking collectives: 44.3 us -> none  [per_device(): whole_diag = lax.all_gather(diag_block, ('row', 'col'), axis=0, tiled=True)]
    select_n x2 -> x0, local copies, waits for them, and re-layouts: 7.09 us -> none  [spread(): jnp.where(lax.axis_index(axis) == holder, block, jnp.zeros_like(block))]
    select_n x1 -> x0, other arithmetic: 5.46 us -> none  [spread(): jnp.where(lax.axis_index(axis) == holder, block, jnp.zeros_like(block))]
  transfers between devices with their start and end apart: 2 -> 3, of which waited for: 2 -> 1; matrix products, arithmetic and copies ran while one was open for 0% -> 0% of each run, Pallas kernels for 0% -> 29%
where the time goes in v1:
time: 210 us
  Pallas kernels  108 us (51%)
  waiting for transfers between devices  82 us (39%)
  between operations  14.1 us (7%)
  local copies, waits for them, and re-layouts  4.25 us (2%)
    all_gather x1, waiting for transfers between devices, per_device(): column_raw = lax.all_gather(column_share, 'row', axis=0, tiled=True)  81.3 us
    pallas_call x1, Pallas kernels, update(): pl.pallas_call(functools.partial(update_kernel, ratio, largest(cols, (512...  47.9 us
    pallas_call x1, Pallas kernels, gather_diag(): pl.pallas_call(functools.partial(gather_diag_kernel, n_row, n_col), out_s...  34.7 us
    pallas_call x1, Pallas kernels, factor(): pl.pallas_call(factor_kernel, out_shape=(square, square, jax.ShapeDtypeSt...  25.3 us
  transfers between devices with their start and end apart: 3, of which 1 were waited for; matrix products, arithmetic and copies ran while one was open for 0% of the time, Pallas kernels for 29%

profile of v1, /device:TPU:0, one launch (start us, length us, event | category | flops | bytes accessed | tf_op | source)
XLA Modules:
  0.0 210.1 jit_solution(1731646768284578807)
XLA Ops:
  7.2 0.0 all-gather.3.cloned.1.call-start
  7.2 0.7 all-gather.3.cloned.1.call-update
  7.9 0.0 all-gather.5.cloned.1.call-start
  7.9 1.8 collective-permute-start
  9.7 0.0 collective-permute-done
  9.7 0.0 copy-start.3
  9.7 0.9 copy-done.3
  10.6 0.0 all-gather.5.cloned.1.call-update
  10.7 34.7 %gather_diag.1 = f32[32,8,256]{2,1,0:T(8,128)} custom-call(f32[8,256]{1,0:T(8,128)} %mine.1), custom_call_target="tpu_custom_call" | custom-call | bytes 16777216 | tf_op jit(solution)/shard_map/gather_diag/pallas_call | solution.py:65
  45.3 0.0 copy-start
  45.3 1.1 copy-done
  46.5 0.0 copy-start.1
  46.5 0.9 copy-done.1
  47.4 25.3 %factor.1 = (f32[256,256]{1,0:T(8,128)S(1)}, f32[256,256]{1,0:T(8,128)S(1)}, f32[768,256]{1,0:T(8,128)}) custom-call(f32[256,256]{1,0:T(8,128)S(1)} %bitcast.1, f32[768,256]{1,0:T(8,128)S(1)} %copy-done), custom_call_target="tpu_custom_call" | custom-call | bytes 134217728 | tf_op jit(solution)/shard_map/factor/pallas_call | solution.py:127
  72.7 0.0 copy-start.2
  72.7 0.7 copy-done.2
  73.4 0.6 constant_dynamic-slice_fusion
  74.0 0.0 all-gather.3.cloned.1.call-done.row_raw
  74.0 81.3 %all-gather.5.cloned.1.call-done.col_raw = f32[6144,256]{1,0:T(8,128)} async-done(((f32[768,256]{1,0:T(8,128)}), f32[6144,256]{1,0:T(8,128)}) %all-gather.5.cloned.1.call-update) | async-done | bytes 6291472 | tf_op jit(solution)/shard_map/all_gather | solution.py:203
  155.3 47.9 %update.1 = bf16[3072,6144]{1,0:T(8,128)(2,1)} custom-call(f32[3072,256]{1,0:T(8,128)} %all-gather.3.cloned.1.call-done.row_raw, f32[6144,256]{1,0:T(8,128)} %all-gather.5.cloned.1.call-done.col_raw, f32[256,256]{1,0:T(8,128)} %copy-done.2, bf16[3072,6144]{1,0:T(8,128)(2,1)} %trailing.1), custom_call_target="tpu_custom_call" | custom-call | flops 28991029248 | bytes 75497472 | tf_op jit(solution)/shard_map/update/pallas_call | solution.py:173
Async XLA Ops:
  7.2 66.9 %all-gather.3.cloned.1.call-start = ((), (), s32[]{:S(2)}) async-start(), calls=%async_computation | async-start | bytes 3932160 | tf_op jit(solution)/shard_map/all_gather | solution.py:204
  7.9 147.4 %all-gather.5.cloned.1.call-start = ((), (), s32[]{:S(2)}) async-start(), calls=%async_computation.1 | async-start | bytes 7077888 | tf_op jit(solution)/shard_map/all_gather | solution.py:203
  7.9 1.8 collective-permute-start
  9.7 0.9 copy-start.3
  45.3 1.1 copy-start
  46.5 0.9 copy-start.1
  72.7 0.7 copy-start.2
Sparse Core Ops, SparseCore 0:
  9.6 42.0 all-gather.2
  54.4 100.9 all-gather.4

commit v2 on v1

--- a/solution.py
+++ b/solution.py
@@ -2,6 +2,7 @@
 
 import jax
 import jax.numpy as jnp
+import numpy as np
 from jax import lax
 from jax.experimental import pallas as pl
 from jax.experimental.pallas import tpu as pltpu
@@ -190,6 +191,135 @@
     )(row_raw, col_raw, inverse, trailing)
 
 
+def left_kernel(row_raw, inverse, left):
+    inverse_parts = split_three(inverse[...], 1, True)
+    left[...] = split_three(
+        dot_last(split_three(row_raw[...], 1, False), inverse_parts), 1, True
+    )
+
+
+def make_left(row_raw, inverse):
+    rows, width = row_raw.shape
+    tile = largest(rows, (768, 512, 256))
+    return pl.pallas_call(
+        left_kernel,
+        grid=(rows // tile,),
+        out_shape=jax.ShapeDtypeStruct((rows, 3 * width), jnp.bfloat16),
+        in_specs=[
+            pl.BlockSpec((tile, width), lambda r: (r, 0)),
+            pl.BlockSpec((width, width), lambda r: (0, 0)),
+        ],
+        out_specs=pl.BlockSpec((tile, 3 * width), lambda r: (r, 0)),
+        compiler_params=pltpu.CompilerParams(vmem_limit_bytes=24 * MIB),
+        cost_estimate=pl.CostEstimate(
+            flops=6 * rows * width * width, bytes_accessed=10 * rows * width, transcendentals=0
+        ),
+        name="left",
+    )(row_raw, inverse)
+
+
+def strips_kernel(shares, per_share, step_rows, *refs):
+    raws = refs[1 : 1 + shares]
+    left, inverse, trailing = refs[1 + shares : 4 + shares]
+    out, right = refs[-2:]
+    step = pl.program_id(0)
+    inverse_parts = split_three(inverse[...], 1, True)
+    for number, raw in enumerate(raws):
+
+        @pl.when(step // per_share == number)
+        def _():
+            first = pl.multiple_of((step - number * per_share) * BLOCK, BLOCK)
+            rows = raw[pl.ds(first, BLOCK), :]
+            right[...] = split_three(
+                dot_last(inverse_parts, split_three(rows, 1, False)), 0, False
+            )
+
+    for start in range(0, trailing.shape[0], step_rows):
+        rows = slice(start, start + step_rows)
+        product = jnp.dot(left[rows, :], right[...], preferred_element_type=jnp.float32)
+        out[rows, :] = (trailing[rows, :].astype(jnp.float32) - product).astype(jnp.bfloat16)
+
+
+def update_strips(columns, raws, left, inverse, trailing, out):
+    rows = trailing.shape[0]
+    width = inverse.shape[0]
+    per_share = raws[0].shape[0] // BLOCK
+    steps = len(raws) * per_share
+    strip = pl.BlockSpec((rows, BLOCK), lambda k, columns: (0, columns[k]))
+    whole = pl.BlockSpec(memory_space=pltpu.VMEM)
+    operands = [columns, *raws, left, inverse, trailing]
+    in_specs = [whole] * (len(raws) + 2) + [strip]
+    aliases = {}
+    if out is not None:
+        aliases = {len(operands): 0}
+        operands.append(out)
+        in_specs.append(pl.BlockSpec(memory_space=pl.ANY))
+    return pl.pallas_call(
+        functools.partial(strips_kernel, len(raws), per_share, largest(rows, (512, 256))),
+        grid_spec=pltpu.PrefetchScalarGridSpec(
+            num_scalar_prefetch=1,
+            grid=(steps,),
+            in_specs=in_specs,
+            out_specs=strip,
+            scratch_shapes=[pltpu.VMEM((3 * width, BLOCK), jnp.bfloat16)],
+        ),
+        out_shape=jax.ShapeDtypeStruct(trailing.shape, jnp.bfloat16),
+        input_output_aliases=aliases,
+        compiler_params=pltpu.CompilerParams(vmem_limit_bytes=32 * MIB),
+        cost_estimate=pl.CostEstimate(
+            flops=6 * rows * steps * BLOCK * width,
+            bytes_accessed=4 * rows * steps * BLOCK,
+            transcendentals=0,
+        ),
+        name="strips",
+    )(*operands)
+
+
+def ring_tables(n_row, n_col, per_share):
+    ring = list(range(0, n_row, 2)) + list(range(n_row - 1, 0, -2))
+    table = np.zeros((n_row, n_row, per_share), np.int32)
+    for place, row in enumerate(ring):
+        for distance in range(n_row):
+            turn, share = divmod(ring[(place - distance) % n_row], n_col)
+            for q in range(per_share):
+                table[row, distance, q] = (share * per_share + q) * (n_row // n_col) + turn
+    forward = [(ring[p], ring[(p + 1) % n_row]) for p in range(n_row)]
+    return forward, [(b, a) for a, b in forward], table
+
+
+def ring_update(share, whole_diag, panel, trailing):
+    n_row, n_col = lax.axis_size("row"), lax.axis_size("col")
+    per_share = share.shape[0] // BLOCK
+    forward, backward, table = ring_tables(n_row, n_col, per_share)
+    columns = lax.dynamic_index_in_dim(
+        jnp.asarray(table), lax.axis_index("row"), 0, keepdims=False
+    )
+    row_raw = lax.all_gather(panel, "col", axis=0, tiled=True)
+    ahead = lax.ppermute(share, "row", forward)
+    behind = lax.ppermute(share, "row", backward)
+    lower, inverse, panel_factor = factor(whole_diag, panel)
+    ahead, behind, inverse = lax.optimization_barrier((ahead, behind, inverse))
+    left = make_left(row_raw, inverse)
+    out, ready, numbers = None, [share], [0]
+    middle, half = n_row // 2, share.shape[0] // 2
+    for distance in range(1, middle + 1):
+        ready, numbers = ready + [ahead, behind], numbers + [distance, n_row - distance]
+        if distance < middle - 1:
+            ahead = lax.ppermute(ahead, "row", forward)
+            behind = lax.ppermute(behind, "row", backward)
+        elif distance == middle - 1:
+            ahead = lax.ppermute(ahead[:half], "row", forward)
+            behind = lax.ppermute(behind[half:], "row", backward)
+        else:
+            ready, numbers = [jnp.concatenate([ahead, behind])], [middle]
+        wanted = jnp.concatenate([columns[number] for number in numbers])
+        out = update_strips(wanted, ready, left, inverse, trailing, out)
+        if distance < middle:
+            ahead, behind, out = lax.optimization_barrier((ahead, behind, out))
+        ready, numbers = [], []
+    return lower, panel_factor, out
+
+
 def per_device(diag_block, panel, trailing):
     n_row, n_col = lax.axis_size("row"), lax.axis_size("col")
     ratio = n_row // n_col
@@ -200,15 +330,20 @@
                 source = (turn * n_col + a) * n_col + b
                 swap.append((source, (turn * n_col + b) * n_col + a))
     column_share = lax.ppermute(panel, ("row", "col"), swap)
-    column_raw = lax.all_gather(column_share, "row", axis=0, tiled=True)
-    row_raw = lax.all_gather(panel, "col", axis=0, tiled=True)
-
     whole_diag = gather_diag(diag_block, n_row, n_col)
-    lower, inverse, panel_factor = factor(whole_diag, panel)
+    if panel.shape[0] % BLOCK == 0 and n_row % 2 == 0 and n_row >= 4:
+        column_share, whole_diag = lax.optimization_barrier((column_share, whole_diag))
+        lower, panel_factor, trailing_out = ring_update(
+            column_share, whole_diag, panel, trailing
+        )
+    else:
+        column_raw = lax.all_gather(column_share, "row", axis=0, tiled=True)
+        row_raw = lax.all_gather(panel, "col", axis=0, tiled=True)
+        lower, inverse, panel_factor = factor(whole_diag, panel)
+        trailing_out = update(row_raw, column_raw, inverse, trailing, ratio)
     share = diag_block.shape[0]
     me = lax.axis_index(("row", "col"))
     factor_rows = lax.dynamic_slice_in_dim(lower, me * share, share, 0)
-    trailing_out = update(row_raw, column_raw, inverse, trailing, ratio)
     return (factor_rows, panel_factor, trailing_out)
 
 

time: 210 us -> 149 us (0.71)
  waiting for transfers between devices: 82 us -> 3.63 us
  starting transfers between devices: 1.87 us -> 10.3 us
  Pallas kernels: 108 us -> 113 us
  local copies, waits for them, and re-layouts: 4.25 us -> 6.71 us
    all_gather x2 -> x1, waiting for transfers between devices: 81.3 us -> 0.01 us  [ring_update(): row_raw = lax.all_gather(panel, 'col', axis=0, tiled=True)]
    pallas_call x1 -> x5, Pallas kernels: 47.9 us -> 59.4 us  [the longest x4 57.3 us: update_strips(): pl.pallas_call(functools.partial(strips_kernel, len(raws), per_share, lar...]
    ppermute x0 -> x8, starting transfers between devices: none -> 8.47 us  [the longest x2 3.66 us: ring_update(): ahead = lax.ppermute(ahead, 'row', forward)]
    pallas_call x1, Pallas kernels: 34.7 us -> 27.8 us  [gather_diag(): pl.pallas_call(functools.partial(gather_diag_kernel, n_row, n_col), out_s...]
    ppermute x0 -> x8, waiting for transfers between devices: none -> 2.95 us  [the longest x2 1.57 us: ring_update(): behind = lax.ppermute(behind, 'row', backward)]
  transfers between devices with their start and end apart: 3 -> 10, of which waited for: 1 -> 2; matrix products, arithmetic and copies ran while one was open for 0% -> 2% of each run, Pallas kernels for 29% -> 70%
where the time goes in v2:
time: 149 us; the launch traced here: 148 us
  Pallas kernels  113 us (76%)
  between operations  14.1 us (9%)
  starting transfers between devices  10.3 us (7%)
  local copies, waits for them, and re-layouts  6.71 us (5%)
  waiting for transfers between devices  3.63 us (2%)
    pallas_call x4, Pallas kernels, update_strips(): pl.pallas_call(functools.partial(strips_kernel, len(raws), per_share, lar...  57.3 us
    pallas_call x1, Pallas kernels, gather_diag(): pl.pallas_call(functools.partial(gather_diag_kernel, n_row, n_col), out_s...  27.8 us
    pallas_call x1, Pallas kernels, factor(): pl.pallas_call(factor_kernel, out_shape=(square, square, jax.ShapeDtypeSt...  25.3 us
    unnamed x8, local copies, waits for them, and re-layouts  4.67 us
    ppermute x2, starting transfers between devices, ring_update(): ahead = lax.ppermute(ahead, 'row', forward)  3.66 us
  transfers between devices with their start and end apart: 10, of which 2 were waited for; matrix products, arithmetic and copies ran while one was open for 2% of the time, Pallas kernels for 70%

profile of v2, /device:TPU:0, one launch (start us, length us, event | category | flops | bytes accessed | tf_op | source)
XLA Modules:
  0.0 147.5 jit_solution(6534291041742448419)
XLA Ops:
  7.2 0.0 all-gather.2.cloned.1.call-start
  7.2 0.7 all-gather.2.cloned.1.call-update
  7.9 1.8 %collective-permute-start = (f32[768,256]{1,0:T(8,128)}, f32[768,256]{1,0:T(8,128)S(1)}, u32[]{:S(2)}, u32[]{:S(2)}) collective-permute-start(f32[768,256]{1,0:T(8,128)} %panel.1), channel_id=1, source_target_pairs={{0,0},{1,4},{2,8},{3,12},{4,1},{5,5},{6,9},{7,13},{8,2},{9,6},{10,... | collective-permute-start | bytes 2359304 | tf_op jit(solution)/shard_map/ppermute | solution.py:332
  9.7 27.8 %gather_diag.1 = f32[32,8,256]{2,1,0:T(8,128)} custom-call(f32[8,256]{1,0:T(8,128)} %mine.1), custom_call_target="tpu_custom_call" | custom-call | bytes 16777216 | tf_op jit(solution)/shard_map/gather_diag/pallas_call | solution.py:66
  37.5 0.0 collective-permute-done.refs_1_
  37.5 2.2 %collective-permute-start.2 = (f32[768,256]{1,0:T(8,128)S(1)}, f32[768,256]{1,0:T(8,128)S(1)}, u32[]{:S(2)}, u32[]{:S(2)}) collective-permute-start(f32[768,256]{1,0:T(8,128)S(1)} %collective-permute-done.refs_1_), channel_id=1, source_target_pairs={{8,0},{16,8},{24,16},{28,24},{20,28},{12,20},{4,12},{0,4},{9,1},{1... | collective-permute-start | bytes 2359304 | tf_op jit(solution)/shard_map/ppermute | solution.py:299
  39.7 0.0 collective-permute-start.1
  39.7 0.7 constant_dynamic-slice_fusion
  40.4 0.1 pad_add_fusion.2.refs_0_
  40.5 0.1 pad_add_fusion.1.refs_0_
  40.6 0.1 pad_add_fusion.refs_0_
  40.6 0.0 copy-start
  40.6 1.1 copy-done
  41.8 0.0 copy-start.2
  41.8 0.9 copy-done.2
  42.7 25.3 %factor.1 = (f32[256,256]{1,0:T(8,128)S(1)}, f32[256,256]{1,0:T(8,128)S(1)}, f32[768,256]{1,0:T(8,128)}) custom-call(f32[256,256]{1,0:T(8,128)S(1)} %bitcast.17, f32[768,256]{1,0:T(8,128)S(1)} %copy-done), custom_call_target="tpu_custom_call" | custom-call | bytes 134217728 | tf_op jit(solution)/shard_map/factor/pallas_call | solution.py:128
  68.0 0.0 copy-start.3
  68.0 0.7 copy-done.3
  68.7 0.0 collective-permute-done.2.refs_3_
  68.7 0.0 collective-permute-done.1.refs_2_
  68.7 1.8 %collective-permute-start.3 = (f32[768,256]{1,0:T(8,128)S(1)}, f32[768,256]{1,0:T(8,128)S(1)}, u32[]{:S(2)}, u32[]{:S(2)}) collective-permute-start(f32[768,256]{1,0:T(8,128)S(1)} %collective-permute-done.1.refs_2_), channel_id=1, source_target_pairs={{0,8},{8,16},{16,24},{24,28},{28,20},{20,12},{12,4},{4,0},{1,9},{9... | collective-permute-start | bytes 2359304 | tf_op jit(solution)/shard_map/ppermute | solution.py:308
  70.6 0.3 collective-permute-start.4
  70.8 0.0 all-gather.2.cloned.1.call-done.row_raw
  70.8 0.0 copy-start.1
  70.8 1.9 %copy-done.1 = f32[3072,256]{1,0:T(8,128)S(1)} copy-done((f32[3072,256]{1,0:T(8,128)S(1)}, f32[3072,256]{1,0:T(8,128)}, u32[]{:S(2)}) %copy-start.1) | copy-done | bytes 3145752
  72.7 2.1 %left.1.refs_4_.refs_3_.refs_2_ = bf16[3072,768]{1,0:T(8,128)(2,1)S(1)} custom-call(f32[3072,256]{1,0:T(8,128)S(1)} %copy-done.1, f32[256,256]{1,0:T(8,128)S(1)} %get-tuple-element.27.inverse.refs_5_.refs_4_.refs_3_), custom_call_target="tpu_custom_call" | custom-call | flops 1207959552 | bytes 7864320 | tf_op jit(solution)/shard_map/left/pallas_call | solution.py:204
  74.8 20.0 %strips.4.refs_6_ = bf16[3072,6144]{1,0:T(8,128)(2,1)} custom-call(s32[9]{0:T(128)S(1)} %pad_add_fusion.refs_0_, f32[768,256]{1,0:T(8,128)S(1)} %collective-permute-done.refs_1_, f32[768,256]{1,0:T(8,128)S(1)} %collective-permute-done.1.refs_2_, f32[768,256]{1,0:T(8,128)S(1)} %collective-permute-done.2.refs_3_, ...), custom_call_target="tpu_custom_call" | custom-call | flops 10871635968 | bytes 28311552 | tf_op jit(solution)/shard_map/strips/pallas_call | solution.py:257
  94.8 0.0 collective-permute-done.3.refs_1_
  94.8 0.0 collective-permute-done.4.refs_2_
  94.8 1.8 %collective-permute-start.5 = (f32[768,256]{1,0:T(8,128)S(1)}, f32[768,256]{1,0:T(8,128)S(1)}, u32[]{:S(2)}, u32[]{:S(2)}) collective-permute-start(f32[768,256]{1,0:T(8,128)S(1)} %collective-permute-done.3.refs_1_), channel_id=1, source_target_pairs={{0,8},{8,16},{16,24},{24,28},{28,20},{20,12},{12,4},{4,0},{1,9},{9... | collective-permute-start | bytes 2359304 | tf_op jit(solution)/shard_map/ppermute | solution.py:308
  96.6 0.3 collective-permute-start.6
  96.9 1.3 constant_dynamic-slice_fusion.1
  98.2 14.5 %strips.5.refs_6_ = bf16[3072,6144]{1,0:T(8,128)(2,1)} custom-call(s32[6]{0:T(128)S(1)} %pad_add_fusion.1.refs_0_, f32[768,256]{1,0:T(8,128)S(1)} %collective-permute-done.3.refs_1_, f32[768,256]{1,0:T(8,128)} %collective-permute-done.4.refs_2_, bf16[3072,768]{1,0:T(8,128)(2,1)S(1)} %left.1.refs_4_.refs_3_.refs_2_, ...), custom_call_target="tpu_custom_call", output_to_operand_aliasing={{}: (6, {})} | custom-call | flops 7247757312 | bytes 18874368 | tf_op jit(solution)/shard_map/strips/pallas_call | solution.py:257
  112.7 1.4 collective-permute-done.5.refs_1_
  114.0 1.6 %collective-permute-done.6.refs_2_ = f32[768,256]{1,0:T(8,128)S(1)} collective-permute-done((f32[768,256]{1,0:T(8,128)}, f32[768,256]{1,0:T(8,128)S(1)}, u32[]{:S(2)}, u32[]{:S(2)}) %collective-permute-start.6) | collective-permute-done | bytes 786464 | tf_op jit(solution)/shard_map/ppermute | solution.py:309
  115.7 1.7 %collective-permute-start.7 = (f32[384,256]{1,0:T(8,128)S(1)}, f32[384,256]{1,0:T(8,128)S(1)}, u32[]{:S(2)}, u32[]{:S(2)}) collective-permute-start(f32[384,256]{1,0:T(8,128)S(1)} %slice.44), channel_id=1, source_target_pairs={{0,8},{8,16},{16,24},{24,28},{28,20},{20,12},{12,4},{4,0},{1,9},{9... | collective-permute-start | bytes 1179656 | tf_op jit(solution)/shard_map/ppermute | solution.py:311
  117.4 0.3 collective-permute-start.8
  117.8 14.2 %strips.6.refs_5_ = bf16[3072,6144]{1,0:T(8,128)(2,1)} custom-call(s32[6]{0:T(128)S(1)} %pad_add_fusion.2.refs_0_, f32[768,256]{1,0:T(8,128)S(1)} %collective-permute-done.5.refs_1_, f32[768,256]{1,0:T(8,128)S(1)} %collective-permute-done.6.refs_2_, bf16[3072,768]{1,0:T(8,128)(2,1)S(1)} %left.1.refs_4_.refs_3_.refs_2_, ...), custom_call_target="tpu_custom_call", output_to_operand_aliasing={{}: (6, {})} | custom-call | flops 7247757312 | bytes 18874368 | tf_op jit(solution)/shard_map/strips/pallas_call | solution.py:257
  132.0 0.0 collective-permute-done.7
  132.0 0.0 collective-permute-done.8
  132.0 0.1 pad_maximum_fusion.refs_1_
  132.1 8.6 %strips.7 = bf16[3072,6144]{1,0:T(8,128)(2,1)} custom-call(s32[3]{0:T(128)S(1)} %get-tuple-element.44.refs_0_, f32[768,256]{1,0:T(8,128)S(1)} %pad_maximum_fusion.refs_1_, bf16[3072,768]{1,0:T(8,128)(2,1)S(1)} %left.1.refs_4_.refs_3_.refs_2_, f32[256,256]{1,0:T(8,128)S(1)} %get-tuple-element.27.inverse.refs_5_.refs_4_.refs_3_, ...), custom_call_target="tpu_custom_call", output_to_operand_aliasing={{}: (5, {})} | custom-call | flops 3623878656 | bytes 9437184 | tf_op jit(solution)/shard_map/strips/pallas_call | solution.py:257
  (3 shorter events, 0.1 us)
Async XLA Ops:
  7.2 63.7 %all-gather.2.cloned.1.call-start = ((), (), s32[]{:S(2)}) async-start(), calls=%async_computation | async-start | bytes 3932160 | tf_op jit(solution)/shard_map/all_gather | solution.py:297
  7.9 29.6 %collective-permute-start = (f32[768,256]{1,0:T(8,128)}, f32[768,256]{1,0:T(8,128)S(1)}, u32[]{:S(2)}, u32[]{:S(2)}) collective-permute-start(f32[768,256]{1,0:T(8,128)} %panel.1), channel_id=1, source_target_pairs={{0,0},{1,4},{2,8},{3,12},{4,1},{5,5},{6,9},{7,13},{8,2},{9,6},{10,... | collective-permute-start | bytes 2359304 | tf_op jit(solution)/shard_map/ppermute | solution.py:332
  37.5 31.2 %collective-permute-start.2 = (f32[768,256]{1,0:T(8,128)S(1)}, f32[768,256]{1,0:T(8,128)S(1)}, u32[]{:S(2)}, u32[]{:S(2)}) collective-permute-start(f32[768,256]{1,0:T(8,128)S(1)} %collective-permute-done.refs_1_), channel_id=1, source_target_pairs={{8,0},{16,8},{24,16},{28,24},{20,28},{12,20},{4,12},{0,4},{9,1},{1... | collective-permute-start | bytes 2359304 | tf_op jit(solution)/shard_map/ppermute | solution.py:299
  39.7 29.0 %collective-permute-start.1 = (f32[768,256]{1,0:T(8,128)S(1)}, f32[768,256]{1,0:T(8,128)S(1)}, u32[]{:S(2)}, u32[]{:S(2)}) collective-permute-start(f32[768,256]{1,0:T(8,128)S(1)} %collective-permute-done.refs_1_), channel_id=1, source_target_pairs={{0,8},{8,16},{16,24},{24,28},{28,20},{20,12},{12,4},{4,0},{1,9},{9... | collective-permute-start | bytes 2359304 | tf_op jit(solution)/shard_map/ppermute | solution.py:298
  40.6 1.1 copy-start
  41.8 0.9 copy-start.2
  68.0 0.7 copy-start.3
  68.7 26.1 %collective-permute-start.3 = (f32[768,256]{1,0:T(8,128)S(1)}, f32[768,256]{1,0:T(8,128)S(1)}, u32[]{:S(2)}, u32[]{:S(2)}) collective-permute-start(f32[768,256]{1,0:T(8,128)S(1)} %collective-permute-done.1.refs_2_), channel_id=1, source_target_pairs={{0,8},{8,16},{16,24},{24,28},{28,20},{20,12},{12,4},{4,0},{1,9},{9... | collective-permute-start | bytes 2359304 | tf_op jit(solution)/shard_map/ppermute | solution.py:308
  70.6 24.2 %collective-permute-start.4 = (f32[768,256]{1,0:T(8,128)S(1)}, f32[768,256]{1,0:T(8,128)}, u32[]{:S(2)}, u32[]{:S(2)}) collective-permute-start(f32[768,256]{1,0:T(8,128)S(1)} %collective-permute-done.2.refs_3_), channel_id=1, source_target_pairs={{8,0},{16,8},{24,16},{28,24},{20,28},{12,20},{4,12},{0,4},{9,1},{1... | collective-permute-start | bytes 2359304 | tf_op jit(solution)/shard_map/ppermute | solution.py:309
  70.8 1.9 %copy-start.1 = (f32[3072,256]{1,0:T(8,128)S(1)}, f32[3072,256]{1,0:T(8,128)}, u32[]{:S(2)}) copy-start(f32[3072,256]{1,0:T(8,128)} %all-gather.2.cloned.1.call-done.row_raw) | copy-start | bytes 9437188
  94.8 19.2 %collective-permute-start.5 = (f32[768,256]{1,0:T(8,128)S(1)}, f32[768,256]{1,0:T(8,128)S(1)}, u32[]{:S(2)}, u32[]{:S(2)}) collective-permute-start(f32[768,256]{1,0:T(8,128)S(1)} %collective-permute-done.3.refs_1_), channel_id=1, source_target_pairs={{0,8},{8,16},{16,24},{24,28},{28,20},{20,12},{12,4},{4,0},{1,9},{9... | collective-permute-start | bytes 2359304 | tf_op jit(solution)/shard_map/ppermute | solution.py:308
  96.6 19.0 %collective-permute-start.6 = (f32[768,256]{1,0:T(8,128)}, f32[768,256]{1,0:T(8,128)S(1)}, u32[]{:S(2)}, u32[]{:S(2)}) collective-permute-start(f32[768,256]{1,0:T(8,128)} %collective-permute-done.4.refs_2_), channel_id=1, source_target_pairs={{8,0},{16,8},{24,16},{28,24},{20,28},{12,20},{4,12},{0,4},{9,1},{1... | collective-permute-start | bytes 2359304 | tf_op jit(solution)/shard_map/ppermute | solution.py:309
  115.7 16.3 %collective-permute-start.7 = (f32[384,256]{1,0:T(8,128)S(1)}, f32[384,256]{1,0:T(8,128)S(1)}, u32[]{:S(2)}, u32[]{:S(2)}) collective-permute-start(f32[384,256]{1,0:T(8,128)S(1)} %slice.44), channel_id=1, source_target_pairs={{0,8},{8,16},{16,24},{24,28},{28,20},{20,12},{12,4},{4,0},{1,9},{9... | collective-permute-start | bytes 1179656 | tf_op jit(solution)/shard_map/ppermute | solution.py:311
  117.4 14.6 %collective-permute-start.8 = (f32[384,256]{1,0:T(8,128)S(1)}, f32[384,256]{1,0:T(8,128)S(1)}, u32[]{:S(2)}, u32[]{:S(2)}) collective-permute-start(f32[384,256]{1,0:T(8,128)S(1)} %slice.45), channel_id=1, source_target_pairs={{8,0},{16,8},{24,16},{28,24},{20,28},{12,20},{4,12},{0,4},{9,1},{1... | collective-permute-start | bytes 1179656 | tf_op jit(solution)/shard_map/ppermute | solution.py:312
Sparse Core Ops, SparseCore 0:
  9.6 41.9 all-gather.1

commit v3 on v2

--- a/solution.py
+++ b/solution.py
@@ -255,7 +255,7 @@
         operands.append(out)
         in_specs.append(pl.BlockSpec(memory_space=pl.ANY))
     return pl.pallas_call(
-        functools.partial(strips_kernel, len(raws), per_share, largest(rows, (512, 256))),
+        functools.partial(strips_kernel, len(raws), per_share, rows),
         grid_spec=pltpu.PrefetchScalarGridSpec(
             num_scalar_prefetch=1,
             grid=(steps,),
@@ -265,7 +265,7 @@
         ),
         out_shape=jax.ShapeDtypeStruct(trailing.shape, jnp.bfloat16),
         input_output_aliases=aliases,
-        compiler_params=pltpu.CompilerParams(vmem_limit_bytes=32 * MIB),
+        compiler_params=pltpu.CompilerParams(vmem_limit_bytes=40 * MIB),
         cost_estimate=pl.CostEstimate(
             flops=6 * rows * steps * BLOCK * width,
             bytes_accessed=4 * rows * steps * BLOCK,
@@ -295,11 +295,12 @@
         jnp.asarray(table), lax.axis_index("row"), 0, keepdims=False
     )
     row_raw = lax.all_gather(panel, "col", axis=0, tiled=True)
+    lower, inverse, panel_factor = factor(whole_diag, panel)
+    share, inverse = lax.optimization_barrier((share, inverse))
     ahead = lax.ppermute(share, "row", forward)
     behind = lax.ppermute(share, "row", backward)
-    lower, inverse, panel_factor = factor(whole_diag, panel)
-    ahead, behind, inverse = lax.optimization_barrier((ahead, behind, inverse))
     left = make_left(row_raw, inverse)
+    ahead, behind, left = lax.optimization_barrier((ahead, behind, left))
     out, ready, numbers = None, [share], [0]
     middle, half = n_row // 2, share.shape[0] // 2
     for distance in range(1, middle + 1):
@@ -329,10 +330,10 @@
             for b in range(n_col):
                 source = (turn * n_col + a) * n_col + b
                 swap.append((source, (turn * n_col + b) * n_col + a))
+    whole_diag = gather_diag(diag_block, n_row, n_col)
+    panel, whole_diag = lax.optimization_barrier((panel, whole_diag))
     column_share = lax.ppermute(panel, ("row", "col"), swap)
-    whole_diag = gather_diag(diag_block, n_row, n_col)
     if panel.shape[0] % BLOCK == 0 and n_row % 2 == 0 and n_row >= 4:
-        column_share, whole_diag = lax.optimization_barrier((column_share, whole_diag))
         lower, panel_factor, trailing_out = ring_update(
             column_share, whole_diag, panel, trailing
         )

time: 149 us -> 147 us (0.987)
  Pallas kernels: 113 us -> 97.7 us
  waiting for transfers between devices: 3.63 us -> 17.3 us
    pallas_call x1, Pallas kernels: 27.8 us -> 13.2 us  [gather_diag(): pl.pallas_call(functools.partial(gather_diag_kernel, n_row, n_col), out_s...]
    ppermute x1, waiting for transfers between devices: 0.01 us -> 6.34 us  [ring_update(): behind = lax.ppermute(share, 'row', backward)]
    all_gather x1, waiting for transfers between devices: 0.01 us -> 5.66 us  [ring_update(): row_raw = lax.all_gather(panel, 'col', axis=0, tiled=True)]
    ppermute x2, starting transfers between devices: 3.66 us -> 1.45 us  [ring_update(): ahead = lax.ppermute(ahead, 'row', forward)]
    ppermute x2, starting transfers between devices: 0.52 us -> 2.65 us  [ring_update(): behind = lax.ppermute(behind, 'row', backward)]
    ppermute x1, waiting for transfers between devices: 0.01 us -> 1.8 us  [ring_update(): ahead = lax.ppermute(share, 'row', forward)]
    unnamed x8 -> x6, local copies, waits for them, and re-layouts: 4.67 us -> 3.97 us
  transfers between devices with their start and end apart: 10 -> 10, of which waited for: 2 -> 5; matrix products, arithmetic and copies ran while one was open for 2% -> 1% of each run, Pallas kernels for 70% -> 52%
where the time goes in v3:
time: 147 us; the launch traced here: 146 us
  Pallas kernels  97.7 us (66%)
  waiting for transfers between devices  17.3 us (12%)
  between operations  14.1 us (10%)
  starting transfers between devices  11.5 us (8%)
  local copies, waits for them, and re-layouts  5.32 us (4%)
    pallas_call x4, Pallas kernels, update_strips(): pl.pallas_call(functools.partial(strips_kernel, len(raws), per_share, row...  57.1 us
    pallas_call x1, Pallas kernels, factor(): pl.pallas_call(factor_kernel, out_shape=(square, square, jax.ShapeDtypeSt...  25.3 us
    pallas_call x1, Pallas kernels, gather_diag(): pl.pallas_call(functools.partial(gather_diag_kernel, n_row, n_col), out_s...  13.2 us
    ppermute x1, waiting for transfers between devices, ring_update(): behind = lax.ppermute(share, 'row', backward)  6.34 us
    all_gather x1, waiting for transfers between devices, ring_update(): row_raw = lax.all_gather(panel, 'col', axis=0, tiled=True)  5.66 us
    unnamed x6, local copies, waits for them, and re-layouts  3.97 us
  transfers between devices with their start and end apart: 10, of which 5 were waited for; matrix products, arithmetic and copies ran while one was open for 1% of the time, Pallas kernels for 52%

profile of v3, /device:TPU:0, one launch (start us, length us, event | category | flops | bytes accessed | tf_op | source)
XLA Modules:
  0.0 146.3 jit_solution(1594849902238583028)
XLA Ops:
  7.2 0.0 all-gather.2.cloned.1.call-start
  7.2 13.2 %gather_diag.1 = f32[32,8,256]{2,1,0:T(8,128)} custom-call(f32[8,256]{1,0:T(8,128)} %mine.1), custom_call_target="tpu_custom_call" | custom-call | bytes 16777216 | tf_op jit(solution)/shard_map/gather_diag/pallas_call | solution.py:66
  20.4 0.0 all-gather.2.cloned.1.call-update
  20.4 1.8 %collective-permute-start = (f32[768,256]{1,0:T(8,128)}, f32[768,256]{1,0:T(8,128)S(1)}, u32[]{:S(2)}, u32[]{:S(2)}) collective-permute-start(f32[768,256]{1,0:T(8,128)} %panel), channel_id=1, source_target_pairs={{0,0},{1,4},{2,8},{3,12},{4,1},{5,5},{6,9},{7,13},{8,2},{9,6},{10,... | collective-permute-start | bytes 2359304 | tf_op jit(solution)/shard_map/ppermute | solution.py:335
  22.2 0.0 copy-start
  22.2 1.1 copy-done
  23.3 0.0 copy-start.2
  23.3 0.9 copy-done.2
  24.3 25.3 %factor.1 = (f32[256,256]{1,0:T(8,128)S(1)}, f32[256,256]{1,0:T(8,128)S(1)}, f32[768,256]{1,0:T(8,128)}) custom-call(f32[256,256]{1,0:T(8,128)S(1)} %bitcast.17, f32[768,256]{1,0:T(8,128)S(1)} %copy-done), custom_call_target="tpu_custom_call" | custom-call | bytes 134217728 | tf_op jit(solution)/shard_map/factor/pallas_call | solution.py:128
  49.6 0.0 collective-permute-done.refs_1_
  49.6 2.4 %collective-permute-start.2 = (f32[768,256]{1,0:T(8,128)S(1)}, f32[768,256]{1,0:T(8,128)S(1)}, u32[]{:S(2)}, u32[]{:S(2)}) collective-permute-start(f32[768,256]{1,0:T(8,128)S(1)} %collective-permute-done.refs_1_), channel_id=1, source_target_pairs={{8,0},{16,8},{24,16},{28,24},{20,28},{12,20},{4,12},{0,4},{9,1},{1... | collective-permute-start | bytes 2359304 | tf_op jit(solution)/shard_map/ppermute | solution.py:301
  52.0 1.1 collective-permute-start.1
  53.1 0.7 constant_dynamic-slice_fusion
  53.8 0.1 pad_add_fusion.2.refs_0_
  53.9 0.1 pad_add_fusion.refs_0_
  54.0 0.6 constant_dynamic-slice_fusion.1
  54.6 5.7 %all-gather.2.cloned.1.call-done.row_raw = f32[3072,256]{1,0:T(8,128)} async-done(((f32[768,256]{1,0:T(8,128)}), f32[3072,256]{1,0:T(8,128)}) %all-gather.2.cloned.1.call-update) | async-done | bytes 3145744 | tf_op jit(solution)/shard_map/all_gather | solution.py:297
  60.3 0.0 copy-start.1
  60.3 1.9 %copy-done.1 = f32[3072,256]{1,0:T(8,128)S(1)} copy-done((f32[3072,256]{1,0:T(8,128)S(1)}, f32[3072,256]{1,0:T(8,128)}, u32[]{:S(2)}) %copy-start.1) | copy-done | bytes 3145752
  62.1 2.1 %left.1.refs_4_.refs_3_.refs_2_ = bf16[3072,768]{1,0:T(8,128)(2,1)S(1)} custom-call(f32[3072,256]{1,0:T(8,128)S(1)} %copy-done.1, f32[256,256]{1,0:T(8,128)S(1)} %get-tuple-element.28.inverse.refs_5_.refs_4_.refs_3_), custom_call_target="tpu_custom_call" | custom-call | flops 1207959552 | bytes 7864320 | tf_op jit(solution)/shard_map/left/pallas_call | solution.py:204
  64.3 6.3 %collective-permute-done.2.refs_3_ = f32[768,256]{1,0:T(8,128)S(1)} collective-permute-done((f32[768,256]{1,0:T(8,128)S(1)}, f32[768,256]{1,0:T(8,128)S(1)}, u32[]{:S(2)}, u32[]{:S(2)}) %collective-permute-start.2) | collective-permute-done | bytes 786464 | tf_op jit(solution)/shard_map/ppermute | solution.py:301
  70.6 1.8 %collective-permute-done.1.refs_2_ = f32[768,256]{1,0:T(8,128)S(1)} collective-permute-done((f32[768,256]{1,0:T(8,128)S(1)}, f32[768,256]{1,0:T(8,128)S(1)}, u32[]{:S(2)}, u32[]{:S(2)}) %collective-permute-start.1) | collective-permute-done | bytes 786464 | tf_op jit(solution)/shard_map/ppermute | solution.py:300
  72.4 0.5 collective-permute-start.3
  73.0 1.5 %collective-permute-start.4 = (f32[768,256]{1,0:T(8,128)S(1)}, f32[768,256]{1,0:T(8,128)S(1)}, u32[]{:S(2)}, u32[]{:S(2)}) collective-permute-start(f32[768,256]{1,0:T(8,128)S(1)} %collective-permute-done.2.refs_3_), channel_id=1, source_target_pairs={{8,0},{16,8},{24,16},{28,24},{20,28},{12,20},{4,12},{0,4},{9,1},{1... | collective-permute-start | bytes 2359304 | tf_op jit(solution)/shard_map/ppermute | solution.py:310
  74.5 20.0 %strips.4.refs_6_ = bf16[3072,6144]{1,0:T(8,128)(2,1)} custom-call(s32[9]{0:T(128)S(1)} %pad_add_fusion.refs_0_, f32[768,256]{1,0:T(8,128)S(1)} %collective-permute-done.refs_1_, f32[768,256]{1,0:T(8,128)S(1)} %collective-permute-done.1.refs_2_, f32[768,256]{1,0:T(8,128)S(1)} %collective-permute-done.2.refs_3_, ...), custom_call_target="tpu_custom_call" | custom-call | flops 10871635968 | bytes 28311552 | tf_op jit(solution)/shard_map/strips/pallas_call | solution.py:257
  94.4 0.0 collective-permute-done.3.refs_1_
  94.4 0.0 collective-permute-done.4.refs_2_
  94.4 0.9 collective-permute-start.5
  95.4 1.2 collective-permute-start.6
  96.5 0.1 pad_add_fusion.1.refs_0_
  96.6 14.3 %strips.5.refs_6_ = bf16[3072,6144]{1,0:T(8,128)(2,1)} custom-call(s32[6]{0:T(128)S(1)} %pad_add_fusion.1.refs_0_, f32[768,256]{1,0:T(8,128)S(1)} %collective-permute-done.3.refs_1_, f32[768,256]{1,0:T(8,128)S(1)} %collective-permute-done.4.refs_2_, bf16[3072,768]{1,0:T(8,128)(2,1)S(1)} %left.1.refs_4_.refs_3_.refs_2_, ...), custom_call_target="tpu_custom_call", output_to_operand_aliasing={{}: (6, {})} | custom-call | flops 7247757312 | bytes 18874368 | tf_op jit(solution)/shard_map/strips/pallas_call | solution.py:257
  110.9 2.4 %collective-permute-done.5.refs_1_ = f32[768,256]{1,0:T(8,128)S(1)} collective-permute-done((f32[768,256]{1,0:T(8,128)S(1)}, f32[768,256]{1,0:T(8,128)S(1)}, u32[]{:S(2)}, u32[]{:S(2)}) %collective-permute-start.5) | collective-permute-done | bytes 786464 | tf_op jit(solution)/shard_map/ppermute | solution.py:309
  113.2 1.2 collective-permute-done.6.refs_2_
  114.4 1.8 %collective-permute-start.7 = (f32[384,256]{1,0:T(8,128)S(1)}, f32[384,256]{1,0:T(8,128)S(1)}, u32[]{:S(2)}, u32[]{:S(2)}) collective-permute-start(f32[384,256]{1,0:T(8,128)S(1)} %slice.44), channel_id=1, source_target_pairs={{0,8},{8,16},{16,24},{24,28},{28,20},{20,12},{12,4},{4,0},{1,9},{9... | collective-permute-start | bytes 1179656 | tf_op jit(solution)/shard_map/ppermute | solution.py:312
  116.2 0.3 collective-permute-start.8
  116.5 14.3 %strips.6.refs_5_ = bf16[3072,6144]{1,0:T(8,128)(2,1)} custom-call(s32[6]{0:T(128)S(1)} %pad_add_fusion.2.refs_0_, f32[768,256]{1,0:T(8,128)S(1)} %collective-permute-done.5.refs_1_, f32[768,256]{1,0:T(8,128)S(1)} %collective-permute-done.6.refs_2_, bf16[3072,768]{1,0:T(8,128)(2,1)S(1)} %left.1.refs_4_.refs_3_.refs_2_, ...), custom_call_target="tpu_custom_call", output_to_operand_aliasing={{}: (6, {})} | custom-call | flops 7247757312 | bytes 18874368 | tf_op jit(solution)/shard_map/strips/pallas_call | solution.py:257
  130.8 0.0 collective-permute-done.7
  130.8 0.0 collective-permute-done.8
  130.8 0.1 pad_maximum_fusion.refs_1_
  130.8 8.6 %strips.7 = bf16[3072,6144]{1,0:T(8,128)(2,1)} custom-call(s32[3]{0:T(128)S(1)} %get-tuple-element.48.refs_0_, f32[768,256]{1,0:T(8,128)S(1)} %pad_maximum_fusion.refs_1_, bf16[3072,768]{1,0:T(8,128)(2,1)S(1)} %left.1.refs_4_.refs_3_.refs_2_, f32[256,256]{1,0:T(8,128)S(1)} %get-tuple-element.28.inverse.refs_5_.refs_4_.refs_3_, ...), custom_call_target="tpu_custom_call", output_to_operand_aliasing={{}: (5, {})} | custom-call | flops 3623878656 | bytes 9437184 | tf_op jit(solution)/shard_map/strips/pallas_call | solution.py:257
  (3 shorter events, 0.1 us)
Async XLA Ops:
  7.2 53.1 %all-gather.2.cloned.1.call-start = ((), (), s32[]{:S(2)}) async-start(), calls=%async_computation | async-start | bytes 3932160 | tf_op jit(solution)/shard_map/all_gather | solution.py:297
  20.4 29.2 %collective-permute-start = (f32[768,256]{1,0:T(8,128)}, f32[768,256]{1,0:T(8,128)S(1)}, u32[]{:S(2)}, u32[]{:S(2)}) collective-permute-start(f32[768,256]{1,0:T(8,128)} %panel), channel_id=1, source_target_pairs={{0,0},{1,4},{2,8},{3,12},{4,1},{5,5},{6,9},{7,13},{8,2},{9,6},{10,... | collective-permute-start | bytes 2359304 | tf_op jit(solution)/shard_map/ppermute | solution.py:335
  22.2 1.1 copy-start
  23.3 0.9 copy-start.2
  49.6 21.0 %collective-permute-start.2 = (f32[768,256]{1,0:T(8,128)S(1)}, f32[768,256]{1,0:T(8,128)S(1)}, u32[]{:S(2)}, u32[]{:S(2)}) collective-permute-start(f32[768,256]{1,0:T(8,128)S(1)} %collective-permute-done.refs_1_), channel_id=1, source_target_pairs={{8,0},{16,8},{24,16},{28,24},{20,28},{12,20},{4,12},{0,4},{9,1},{1... | collective-permute-start | bytes 2359304 | tf_op jit(solution)/shard_map/ppermute | solution.py:301
  52.0 20.4 %collective-permute-start.1 = (f32[768,256]{1,0:T(8,128)S(1)}, f32[768,256]{1,0:T(8,128)S(1)}, u32[]{:S(2)}, u32[]{:S(2)}) collective-permute-start(f32[768,256]{1,0:T(8,128)S(1)} %collective-permute-done.refs_1_), channel_id=1, source_target_pairs={{0,8},{8,16},{16,24},{24,28},{28,20},{20,12},{12,4},{4,0},{1,9},{9... | collective-permute-start | bytes 2359304 | tf_op jit(solution)/shard_map/ppermute | solution.py:300
  60.3 1.9 %copy-start.1 = (f32[3072,256]{1,0:T(8,128)S(1)}, f32[3072,256]{1,0:T(8,128)}, u32[]{:S(2)}) copy-start(f32[3072,256]{1,0:T(8,128)} %all-gather.2.cloned.1.call-done.row_raw) | copy-start | bytes 9437188
  72.4 22.0 %collective-permute-start.3 = (f32[768,256]{1,0:T(8,128)S(1)}, f32[768,256]{1,0:T(8,128)S(1)}, u32[]{:S(2)}, u32[]{:S(2)}) collective-permute-start(f32[768,256]{1,0:T(8,128)S(1)} %collective-permute-done.1.refs_2_), channel_id=1, source_target_pairs={{0,8},{8,16},{16,24},{24,28},{28,20},{20,12},{12,4},{4,0},{1,9},{9... | collective-permute-start | bytes 2359304 | tf_op jit(solution)/shard_map/ppermute | solution.py:309
  73.0 21.5 %collective-permute-start.4 = (f32[768,256]{1,0:T(8,128)S(1)}, f32[768,256]{1,0:T(8,128)S(1)}, u32[]{:S(2)}, u32[]{:S(2)}) collective-permute-start(f32[768,256]{1,0:T(8,128)S(1)} %collective-permute-done.2.refs_3_), channel_id=1, source_target_pairs={{8,0},{16,8},{24,16},{28,24},{20,28},{12,20},{4,12},{0,4},{9,1},{1... | collective-permute-start | bytes 2359304 | tf_op jit(solution)/shard_map/ppermute | solution.py:310
  94.4 18.8 %collective-permute-start.5 = (f32[768,256]{1,0:T(8,128)S(1)}, f32[768,256]{1,0:T(8,128)S(1)}, u32[]{:S(2)}, u32[]{:S(2)}) collective-permute-start(f32[768,256]{1,0:T(8,128)S(1)} %collective-permute-done.3.refs_1_), channel_id=1, source_target_pairs={{0,8},{8,16},{16,24},{24,28},{28,20},{20,12},{12,4},{4,0},{1,9},{9... | collective-permute-start | bytes 2359304 | tf_op jit(solution)/shard_map/ppermute | solution.py:309
  95.4 19.0 %collective-permute-start.6 = (f32[768,256]{1,0:T(8,128)S(1)}, f32[768,256]{1,0:T(8,128)S(1)}, u32[]{:S(2)}, u32[]{:S(2)}) collective-permute-start(f32[768,256]{1,0:T(8,128)S(1)} %collective-permute-done.4.refs_2_), channel_id=1, source_target_pairs={{8,0},{16,8},{24,16},{28,24},{20,28},{12,20},{4,12},{0,4},{9,1},{1... | collective-permute-start | bytes 2359304 | tf_op jit(solution)/shard_map/ppermute | solution.py:310
  114.4 16.3 %collective-permute-start.7 = (f32[384,256]{1,0:T(8,128)S(1)}, f32[384,256]{1,0:T(8,128)S(1)}, u32[]{:S(2)}, u32[]{:S(2)}) collective-permute-start(f32[384,256]{1,0:T(8,128)S(1)} %slice.44), channel_id=1, source_target_pairs={{0,8},{8,16},{16,24},{24,28},{28,20},{20,12},{12,4},{4,0},{1,9},{9... | collective-permute-start | bytes 1179656 | tf_op jit(solution)/shard_map/ppermute | solution.py:312
  116.2 14.6 %collective-permute-start.8 = (f32[384,256]{1,0:T(8,128)S(1)}, f32[384,256]{1,0:T(8,128)S(1)}, u32[]{:S(2)}, u32[]{:S(2)}) collective-permute-start(f32[384,256]{1,0:T(8,128)S(1)} %slice.45), channel_id=1, source_target_pairs={{8,0},{16,8},{24,16},{28,24},{20,28},{12,20},{4,12},{0,4},{9,1},{1... | collective-permute-start | bytes 1179656 | tf_op jit(solution)/shard_map/ppermute | solution.py:313
Sparse Core Ops, SparseCore 0:
  20.5 39.6 all-gather.1

commit v4 on v3

--- a/solution.py
+++ b/solution.py
@@ -300,8 +300,9 @@
     ahead = lax.ppermute(share, "row", forward)
     behind = lax.ppermute(share, "row", backward)
     left = make_left(row_raw, inverse)
-    ahead, behind, left = lax.optimization_barrier((ahead, behind, left))
-    out, ready, numbers = None, [share], [0]
+    out = update_strips(columns[0], [share], left, inverse, trailing, None)
+    ahead, behind, out = lax.optimization_barrier((ahead, behind, out))
+    ready, numbers = [], []
     middle, half = n_row // 2, share.shape[0] // 2
     for distance in range(1, middle + 1):
         ready, numbers = ready + [ahead, behind], numbers + [distance, n_row - distance]

time: 147 us -> 149 us (1.014)
  Pallas kernels: 97.7 us -> 101 us
  waiting for transfers between devices: 17.3 us -> 14.2 us
  starting transfers between devices: 11.5 us -> 13.4 us
    ppermute x1, waiting for transfers between devices: 6.34 us -> 0.01 us  [ring_update(): behind = lax.ppermute(share, 'row', backward)]
    ppermute x2, starting transfers between devices: 1.45 us -> 4.8 us  [ring_update(): ahead = lax.ppermute(ahead, 'row', forward)]
    pallas_call x4 -> x5, Pallas kernels: 57.1 us -> 60 us  [update_strips(): pl.pallas_call(functools.partial(strips_kernel, len(raws), per_share, row...]
    ppermute x2, waiting for transfers between devices: 2.36 us -> 5.07 us  [ring_update(): ahead = lax.ppermute(ahead, 'row', forward)]
    ppermute x2, waiting for transfers between devices: 1.16 us -> 3.15 us  [ring_update(): behind = lax.ppermute(behind, 'row', backward)]
    ppermute x1, waiting for transfers between devices: 1.8 us -> 0.22 us  [ring_update(): ahead = lax.ppermute(share, 'row', forward)]
    ppermute x2, starting transfers between devices: 2.65 us -> 1.14 us  [ring_update(): behind = lax.ppermute(behind, 'row', backward)]
  transfers between devices with their start and end apart: 10 -> 10, of which waited for: 5 -> 6; matrix products, arithmetic and copies ran while one was open for 1% -> 1% of each run, Pallas kernels for 52% -> 53%
where the time goes in v4:
time: 149 us; the launch traced here: 148 us
  Pallas kernels  101 us (68%)
  waiting for transfers between devices  14.2 us (10%)
  between operations  14.1 us (9%)
  starting transfers between devices  13.4 us (9%)
  local copies, waits for them, and re-layouts  5.32 us (4%)
    pallas_call x5, Pallas kernels, update_strips(): pl.pallas_call(functools.partial(strips_kernel, len(raws), per_share, row...  60 us
    pallas_call x1, Pallas kernels, factor(): pl.pallas_call(factor_kernel, out_shape=(square, square, jax.ShapeDtypeSt...  25.3 us
    pallas_call x1, Pallas kernels, gather_diag(): pl.pallas_call(functools.partial(gather_diag_kernel, n_row, n_col), out_s...  13.2 us
    all_gather x1, waiting for transfers between devices, ring_update(): row_raw = lax.all_gather(panel, 'col', axis=0, tiled=True)  5.74 us
    ppermute x2, waiting for transfers between devices, ring_update(): ahead = lax.ppermute(ahead, 'row', forward)  5.07 us
    ppermute x2, starting transfers between devices, ring_update(): ahead = lax.ppermute(ahead, 'row', forward)  4.8 us
    unnamed x6, local copies, waits for them, and re-layouts  3.97 us
    ppermute x2, waiting for transfers between devices, ring_update(): behind = lax.ppermute(behind, 'row', backward)  3.15 us
  transfers between devices with their start and end apart: 10, of which 6 were waited for; matrix products, arithmetic and copies ran while one was open for 1% of the time, Pallas kernels for 53%

profile of v4, /device:TPU:0, one launch (start us, length us, event | category | flops | bytes accessed | tf_op | source)
XLA Modules:
  0.0 147.9 jit_solution(12520716262533380412)
XLA Ops:
  7.2 0.0 all-gather.2.cloned.1.call-start
  7.2 13.2 %gather_diag.1 = f32[32,8,256]{2,1,0:T(8,128)} custom-call(f32[8,256]{1,0:T(8,128)} %mine.1), custom_call_target="tpu_custom_call" | custom-call | bytes 16777216 | tf_op jit(solution)/shard_map/gather_diag/pallas_call | solution.py:66
  20.4 0.0 all-gather.2.cloned.1.call-update
  20.4 1.8 %collective-permute-start = (f32[768,256]{1,0:T(8,128)}, f32[768,256]{1,0:T(8,128)S(1)}, u32[]{:S(2)}, u32[]{:S(2)}) collective-permute-start(f32[768,256]{1,0:T(8,128)} %panel), channel_id=1, source_target_pairs={{0,0},{1,4},{2,8},{3,12},{4,1},{5,5},{6,9},{7,13},{8,2},{9,6},{10,... | collective-permute-start | bytes 2359304 | tf_op jit(solution)/shard_map/ppermute | solution.py:336
  22.2 0.0 copy-start
  22.2 1.1 copy-done
  23.3 0.0 copy-start.2
  23.3 0.9 copy-done.2
  24.3 25.3 %factor.1 = (f32[256,256]{1,0:T(8,128)S(1)}, f32[256,256]{1,0:T(8,128)S(1)}, f32[768,256]{1,0:T(8,128)}) custom-call(f32[256,256]{1,0:T(8,128)S(1)} %bitcast.17, f32[768,256]{1,0:T(8,128)S(1)} %copy-done), custom_call_target="tpu_custom_call" | custom-call | bytes 134217728 | tf_op jit(solution)/shard_map/factor/pallas_call | solution.py:128
  49.6 0.7 constant_dynamic-slice_fusion
  50.3 0.0 collective-permute-done.refs_1_
  50.3 2.4 %collective-permute-start.2 = (f32[768,256]{1,0:T(8,128)S(1)}, f32[768,256]{1,0:T(8,128)S(1)}, u32[]{:S(2)}, u32[]{:S(2)}) collective-permute-start(f32[768,256]{1,0:T(8,128)S(1)} %collective-permute-done.refs_1_), channel_id=1, source_target_pairs={{8,0},{16,8},{24,16},{28,24},{20,28},{12,20},{4,12},{0,4},{9,1},{1... | collective-permute-start | bytes 2359304 | tf_op jit(solution)/shard_map/ppermute | solution.py:301
  52.7 1.1 collective-permute-start.1
  53.8 0.1 pad_add_fusion.2.refs_0_
  53.9 0.6 constant_dynamic-slice_fusion.1
  54.5 5.7 %all-gather.2.cloned.1.call-done.row_raw = f32[3072,256]{1,0:T(8,128)} async-done(((f32[768,256]{1,0:T(8,128)}), f32[3072,256]{1,0:T(8,128)}) %all-gather.2.cloned.1.call-update) | async-done | bytes 3145744 | tf_op jit(solution)/shard_map/all_gather | solution.py:297
  60.3 0.0 copy-start.1
  60.3 1.9 %copy-done.1 = f32[3072,256]{1,0:T(8,128)S(1)} copy-done((f32[3072,256]{1,0:T(8,128)S(1)}, f32[3072,256]{1,0:T(8,128)}, u32[]{:S(2)}) %copy-start.1) | copy-done | bytes 3145752
  62.1 2.1 %left.1.refs_2_.refs_3_ = bf16[3072,768]{1,0:T(8,128)(2,1)S(1)} custom-call(f32[3072,256]{1,0:T(8,128)S(1)} %copy-done.1, f32[256,256]{1,0:T(8,128)S(1)} %get-tuple-element.28.inverse.refs_3_.refs_4_), custom_call_target="tpu_custom_call" | custom-call | flops 1207959552 | bytes 7864320 | tf_op jit(solution)/shard_map/left/pallas_call | solution.py:204
  64.3 8.6 %strips.5.refs_6_ = bf16[3072,6144]{1,0:T(8,128)(2,1)} custom-call(s32[3]{0:T(128)S(1)} %get-tuple-element.47.refs_0_, f32[768,256]{1,0:T(8,128)S(1)} %collective-permute-done.refs_1_, bf16[3072,768]{1,0:T(8,128)(2,1)S(1)} %left.1.refs_2_.refs_3_, f32[256,256]{1,0:T(8,128)S(1)} %get-tuple-element.28.inverse.refs_3_.refs_4_, bf16[3072,6144]{1,0:T(8,128)(2,1)} %refs_4_.3), custom_call_target="tpu_custom_call" | custom-call | flops 3623878656 | bytes 9437184 | tf_op jit(solution)/shard_map/strips/pallas_call | solution.py:257
  72.9 0.0 collective-permute-done.2.refs_2_
  72.9 0.2 collective-permute-done.1.refs_1_
  73.1 3.9 %collective-permute-start.3 = (f32[768,256]{1,0:T(8,128)S(1)}, f32[768,256]{1,0:T(8,128)S(1)}, u32[]{:S(2)}, u32[]{:S(2)}) collective-permute-start(f32[768,256]{1,0:T(8,128)S(1)} %collective-permute-done.1.refs_1_), channel_id=1, source_target_pairs={{0,8},{8,16},{16,24},{24,28},{28,20},{20,12},{12,4},{4,0},{1,9},{9... | collective-permute-start | bytes 2359304 | tf_op jit(solution)/shard_map/ppermute | solution.py:310
  77.0 0.0 collective-permute-start.4
  77.0 0.1 pad_add_fusion.refs_0_
  77.1 14.3 %strips.6.refs_6_ = bf16[3072,6144]{1,0:T(8,128)(2,1)} custom-call(s32[6]{0:T(128)S(1)} %pad_add_fusion.refs_0_, f32[768,256]{1,0:T(8,128)S(1)} %collective-permute-done.1.refs_1_, f32[768,256]{1,0:T(8,128)S(1)} %collective-permute-done.2.refs_2_, bf16[3072,768]{1,0:T(8,128)(2,1)S(1)} %left.1.refs_2_.refs_3_, ...), custom_call_target="tpu_custom_call", output_to_operand_aliasing={{}: (6, {})} | custom-call | flops 7247757312 | bytes 18874368 | tf_op jit(solution)/shard_map/strips/pallas_call | solution.py:257
  91.4 2.9 %collective-permute-done.3.refs_1_ = f32[768,256]{1,0:T(8,128)S(1)} collective-permute-done((f32[768,256]{1,0:T(8,128)S(1)}, f32[768,256]{1,0:T(8,128)S(1)}, u32[]{:S(2)}, u32[]{:S(2)}) %collective-permute-start.3) | collective-permute-done | bytes 786464 | tf_op jit(solution)/shard_map/ppermute | solution.py:310
  94.3 2.2 %collective-permute-done.4.refs_2_ = f32[768,256]{1,0:T(8,128)S(1)} collective-permute-done((f32[768,256]{1,0:T(8,128)S(1)}, f32[768,256]{1,0:T(8,128)S(1)}, u32[]{:S(2)}, u32[]{:S(2)}) %collective-permute-start.4) | collective-permute-done | bytes 786464 | tf_op jit(solution)/shard_map/ppermute | solution.py:311
  96.5 0.9 collective-permute-start.5
  97.3 1.1 collective-permute-start.6
  98.5 0.1 pad_add_fusion.1.refs_0_
  98.6 14.3 %strips.7.refs_6_ = bf16[3072,6144]{1,0:T(8,128)(2,1)} custom-call(s32[6]{0:T(128)S(1)} %pad_add_fusion.1.refs_0_, f32[768,256]{1,0:T(8,128)S(1)} %collective-permute-done.3.refs_1_, f32[768,256]{1,0:T(8,128)S(1)} %collective-permute-done.4.refs_2_, bf16[3072,768]{1,0:T(8,128)(2,1)S(1)} %left.1.refs_2_.refs_3_, ...), custom_call_target="tpu_custom_call", output_to_operand_aliasing={{}: (6, {})} | custom-call | flops 7247757312 | bytes 18874368 | tf_op jit(solution)/shard_map/strips/pallas_call | solution.py:257
  112.8 2.2 %collective-permute-done.5.refs_1_ = f32[768,256]{1,0:T(8,128)S(1)} collective-permute-done((f32[768,256]{1,0:T(8,128)S(1)}, f32[768,256]{1,0:T(8,128)S(1)}, u32[]{:S(2)}, u32[]{:S(2)}) %collective-permute-start.5) | collective-permute-done | bytes 786464 | tf_op jit(solution)/shard_map/ppermute | solution.py:310
  115.0 0.9 collective-permute-done.6.refs_2_
  116.0 1.5 collective-permute-start.7
  117.5 0.6 collective-permute-start.8
  118.1 14.3 %strips.8.refs_5_ = bf16[3072,6144]{1,0:T(8,128)(2,1)} custom-call(s32[6]{0:T(128)S(1)} %pad_add_fusion.2.refs_0_, f32[768,256]{1,0:T(8,128)S(1)} %collective-permute-done.5.refs_1_, f32[768,256]{1,0:T(8,128)S(1)} %collective-permute-done.6.refs_2_, bf16[3072,768]{1,0:T(8,128)(2,1)S(1)} %left.1.refs_2_.refs_3_, ...), custom_call_target="tpu_custom_call", output_to_operand_aliasing={{}: (6, {})} | custom-call | flops 7247757312 | bytes 18874368 | tf_op jit(solution)/shard_map/strips/pallas_call | solution.py:257
  132.4 0.0 collective-permute-done.7
  132.4 0.0 collective-permute-done.8
  132.4 0.1 pad_maximum_fusion.refs_1_
  132.4 8.6 %strips.9 = bf16[3072,6144]{1,0:T(8,128)(2,1)} custom-call(s32[3]{0:T(128)S(1)} %get-tuple-element.48.refs_0_, f32[768,256]{1,0:T(8,128)S(1)} %pad_maximum_fusion.refs_1_, bf16[3072,768]{1,0:T(8,128)(2,1)S(1)} %left.1.refs_2_.refs_3_, f32[256,256]{1,0:T(8,128)S(1)} %get-tuple-element.28.inverse.refs_3_.refs_4_, ...), custom_call_target="tpu_custom_call", output_to_operand_aliasing={{}: (5, {})} | custom-call | flops 3623878656 | bytes 9437184 | tf_op jit(solution)/shard_map/strips/pallas_call | solution.py:257
  (3 shorter events, 0.1 us)
Async XLA Ops:
  7.2 53.1 %all-gather.2.cloned.1.call-start = ((), (), s32[]{:S(2)}) async-start(), calls=%async_computation | async-start | bytes 3932160 | tf_op jit(solution)/shard_map/all_gather | solution.py:297
  20.4 29.9 %collective-permute-start = (f32[768,256]{1,0:T(8,128)}, f32[768,256]{1,0:T(8,128)S(1)}, u32[]{:S(2)}, u32[]{:S(2)}) collective-permute-start(f32[768,256]{1,0:T(8,128)} %panel), channel_id=1, source_target_pairs={{0,0},{1,4},{2,8},{3,12},{4,1},{5,5},{6,9},{7,13},{8,2},{9,6},{10,... | collective-permute-start | bytes 2359304 | tf_op jit(solution)/shard_map/ppermute | solution.py:336
  22.2 1.1 copy-start
  23.3 0.9 copy-start.2
  50.3 22.6 %collective-permute-start.2 = (f32[768,256]{1,0:T(8,128)S(1)}, f32[768,256]{1,0:T(8,128)S(1)}, u32[]{:S(2)}, u32[]{:S(2)}) collective-permute-start(f32[768,256]{1,0:T(8,128)S(1)} %collective-permute-done.refs_1_), channel_id=1, source_target_pairs={{8,0},{16,8},{24,16},{28,24},{20,28},{12,20},{4,12},{0,4},{9,1},{1... | collective-permute-start | bytes 2359304 | tf_op jit(solution)/shard_map/ppermute | solution.py:301
  52.7 20.4 %collective-permute-start.1 = (f32[768,256]{1,0:T(8,128)S(1)}, f32[768,256]{1,0:T(8,128)S(1)}, u32[]{:S(2)}, u32[]{:S(2)}) collective-permute-start(f32[768,256]{1,0:T(8,128)S(1)} %collective-permute-done.refs_1_), channel_id=1, source_target_pairs={{0,8},{8,16},{16,24},{24,28},{28,20},{20,12},{12,4},{4,0},{1,9},{9... | collective-permute-start | bytes 2359304 | tf_op jit(solution)/shard_map/ppermute | solution.py:300
  60.3 1.9 %copy-start.1 = (f32[3072,256]{1,0:T(8,128)S(1)}, f32[3072,256]{1,0:T(8,128)}, u32[]{:S(2)}) copy-start(f32[3072,256]{1,0:T(8,128)} %all-gather.2.cloned.1.call-done.row_raw) | copy-start | bytes 9437188
  73.1 21.1 %collective-permute-start.3 = (f32[768,256]{1,0:T(8,128)S(1)}, f32[768,256]{1,0:T(8,128)S(1)}, u32[]{:S(2)}, u32[]{:S(2)}) collective-permute-start(f32[768,256]{1,0:T(8,128)S(1)} %collective-permute-done.1.refs_1_), channel_id=1, source_target_pairs={{0,8},{8,16},{16,24},{24,28},{28,20},{20,12},{12,4},{4,0},{1,9},{9... | collective-permute-start | bytes 2359304 | tf_op jit(solution)/shard_map/ppermute | solution.py:310
  77.0 19.4 %collective-permute-start.4 = (f32[768,256]{1,0:T(8,128)S(1)}, f32[768,256]{1,0:T(8,128)S(1)}, u32[]{:S(2)}, u32[]{:S(2)}) collective-permute-start(f32[768,256]{1,0:T(8,128)S(1)} %collective-permute-done.2.refs_2_), channel_id=1, source_target_pairs={{8,0},{16,8},{24,16},{28,24},{20,28},{12,20},{4,12},{0,4},{9,1},{1... | collective-permute-start | bytes 2359304 | tf_op jit(solution)/shard_map/ppermute | solution.py:311
  96.5 18.6 %collective-permute-start.5 = (f32[768,256]{1,0:T(8,128)S(1)}, f32[768,256]{1,0:T(8,128)S(1)}, u32[]{:S(2)}, u32[]{:S(2)}) collective-permute-start(f32[768,256]{1,0:T(8,128)S(1)} %collective-permute-done.3.refs_1_), channel_id=1, source_target_pairs={{0,8},{8,16},{16,24},{24,28},{28,20},{20,12},{12,4},{4,0},{1,9},{9... | collective-permute-start | bytes 2359304 | tf_op jit(solution)/shard_map/ppermute | solution.py:310
  97.3 18.6 %collective-permute-start.6 = (f32[768,256]{1,0:T(8,128)S(1)}, f32[768,256]{1,0:T(8,128)S(1)}, u32[]{:S(2)}, u32[]{:S(2)}) collective-permute-start(f32[768,256]{1,0:T(8,128)S(1)} %collective-permute-done.4.refs_2_), channel_id=1, source_target_pairs={{8,0},{16,8},{24,16},{28,24},{20,28},{12,20},{4,12},{0,4},{9,1},{1... | collective-permute-start | bytes 2359304 | tf_op jit(solution)/shard_map/ppermute | solution.py:311
  116.0 16.3 %collective-permute-start.7 = (f32[384,256]{1,0:T(8,128)S(1)}, f32[384,256]{1,0:T(8,128)S(1)}, u32[]{:S(2)}, u32[]{:S(2)}) collective-permute-start(f32[384,256]{1,0:T(8,128)S(1)} %slice.44), channel_id=1, source_target_pairs={{0,8},{8,16},{16,24},{24,28},{28,20},{20,12},{12,4},{4,0},{1,9},{9... | collective-permute-start | bytes 1179656 | tf_op jit(solution)/shard_map/ppermute | solution.py:313
  117.5 14.9 %collective-permute-start.8 = (f32[384,256]{1,0:T(8,128)S(1)}, f32[384,256]{1,0:T(8,128)S(1)}, u32[]{:S(2)}, u32[]{:S(2)}) collective-permute-start(f32[384,256]{1,0:T(8,128)S(1)} %slice.45), channel_id=1, source_target_pairs={{8,0},{16,8},{24,16},{28,24},{20,28},{12,20},{4,12},{0,4},{9,1},{1... | collective-permute-start | bytes 1179656 | tf_op jit(solution)/shard_map/ppermute | solution.py:314
Sparse Core Ops, SparseCore 0:
  20.5 39.6 all-gather.1
